TPU v7x, 32 devices: a whole 2x2x4 slice. The times are simulated.
32 devices in a mesh: uv: 4 (over y, core), channel: 4 (over z), parity: 2 (over x).
Axes of the slice: x: 2, y: 2, z: 4, core: 2. Of those that a mesh axis runs over, the one named last changes fastest.
Arguments:
- visibility: bfloat16 [2, 4, 128, 32, 128], P('parity', 'channel', 'uv'), may hold values from -6 to 6
- kernel: bfloat16 [2, 4, 128, 128, 256], P('parity', 'channel', 'uv'), may hold values from -0.5 to 0.5
- block_tile: int32 [2, 4, 128], P('parity', 'channel', 'uv'), may hold values from 0 to 255, as said below
- block_chan: int32 [2, 4, 128], P('parity', 'channel', 'uv'), may hold values from 0 to 240
- tile_owner: int32 [256], replicated, may hold values from 0 to 3, as said below
- inv_cov: bfloat16 [1024, 1024], replicated, as said below
Outputs:
- cross_power: float32 [1024, 65536], P(None, ('uv', 'channel', 'parity'))
- diff_power: float32 [1024, 65536], P(None, ('uv', 'channel', 'parity'))
Inputs may be any that keep to these rules, and one draw needn't show every extreme that they name: `tile_owner`: each owner index owns exactly 64 tiles. `block_tile`: call slot(t) // 16 the cell group of tile t. Among the 32 blocks of one device (one aligned run along the last dimension), at most 4 name tiles of the same owner and the same cell group. `inv_cov`: entries are finite.
All inputs are finite; a program needn't handle non-finite values.
Results may differ from a plain program's by a relative error of at most 0.0067.
Values may be sent and summed in bfloat16 or wider, within the bound.
A program may use at most 192 MiB of HBM per device.

v0:
```python
import math

import jax
import jax.numpy as jnp
from jax import lax
from jax.sharding import PartitionSpec as P


def delay_table(count):
    indices = jnp.arange(count, dtype=jnp.int32)
    phase_int = indices[:, None] * indices[None, :] % count
    angles = phase_int.astype(jnp.float32) * (2.0 * math.pi / count)
    return jnp.concatenate([jnp.cos(angles), jnp.sin(angles)], axis=0).astype(jnp.bfloat16)


def accumulate(received, row_index, row_total):
    half_width = row_index.shape[1]
    pixels = received.shape[-1]
    values = jnp.moveaxis(received.reshape(-1, 2, half_width, pixels), 1, 0).reshape(2, -1, pixels)
    flat_rows = jnp.clip(row_index, 0, row_total - 1).reshape(-1).astype(jnp.int32)
    row_block = math.gcd(row_total, 512)

    def grid_block(block_index):
        targets = block_index * row_block + jnp.arange(row_block, dtype=jnp.int32)
        onehot = (targets[:, None] == flat_rows[None, :]).astype(jnp.bfloat16)
        summed = jnp.einsum("nm,rmp->rnp", onehot, values, preferred_element_type=jnp.float32)
        return summed.astype(jnp.bfloat16)

    pieces = lax.map(grid_block, jnp.arange(row_total // row_block, dtype=jnp.int32))
    return jnp.moveaxis(pieces, 1, 0).reshape(2, row_total, pixels)


def on_device(visibility, kernel, block_tile, block_chan, tile_owner, inv_cov):
    uv_count = lax.axis_size("uv")
    chan_count = lax.axis_size("channel")
    samples = visibility[0, 0]
    weights = kernel[0, 0]
    tile_ids = block_tile[0, 0]
    starts = block_chan[0, 0]
    blocks = samples.shape[0]
    doubled = samples.shape[1]
    half_width = doubled // 2
    pixels = weights.shape[2]
    channels = inv_cov.shape[0]
    chan_dev = channels // chan_count
    tile_total = tile_owner.shape[0]
    tile_dev = tile_total // uv_count
    group_tiles = tile_dev // chan_count
    dest_count = uv_count * chan_count
    slot_count = max(1, 2 * blocks // dest_count)
    slot_total = dest_count * slot_count
    partials = jnp.einsum(
        "bkv,bvp->bkp", samples, weights, preferred_element_type=jnp.float32
    ).astype(jnp.bfloat16)
    indices = jnp.arange(tile_total, dtype=jnp.int32)
    same_owner = (tile_owner[:, None] == tile_owner[None, :]) & (
        indices[:, None] < indices[None, :]
    )
    tile_slot = jnp.sum(same_owner.astype(jnp.int32), axis=0)
    picked = tile_ids[:, None] == indices[None, :]
    owner_of = jnp.sum(jnp.where(picked, tile_owner[None, :], 0), axis=1)
    slot_of = jnp.sum(jnp.where(picked, tile_slot[None, :], 0), axis=1)
    target = owner_of * chan_count + slot_of // group_tiles
    block_order = jnp.arange(blocks, dtype=jnp.int32)
    earlier = (target[:, None] == target[None, :]) & (block_order[:, None] < block_order[None, :])
    rank_of = jnp.sum(earlier.astype(jnp.int32), axis=0)
    position = target * slot_count + rank_of
    outgoing = jnp.zeros((slot_total, doubled, pixels), jnp.bfloat16).at[position].set(partials)
    out_slot = jnp.zeros((slot_total,), jnp.int32).at[position].set(slot_of)
    out_chan = (
        jnp.zeros((slot_total,), jnp.int32)
        .at[position]
        .set(starts + lax.axis_index("channel") * chan_dev)
    )
    chan_offsets = jnp.arange(half_width, dtype=jnp.int32)
    received, got_slot, got_chan = (
        lax.all_to_all(
            lax.all_to_all(
                outgoing.reshape(uv_count, chan_count, slot_count, doubled, pixels),
                "uv",
                split_axis=0,
                concat_axis=0,
                tiled=True,
            ),
            "channel",
            split_axis=1,
            concat_axis=1,
            tiled=True,
        ),
        lax.all_to_all(
            lax.all_to_all(
                out_slot.reshape(uv_count, chan_count, slot_count),
                "uv",
                split_axis=0,
                concat_axis=0,
                tiled=True,
            ),
            "channel",
            split_axis=1,
            concat_axis=1,
            tiled=True,
        ),
        lax.all_to_all(
            lax.all_to_all(
                out_chan.reshape(uv_count, chan_count, slot_count),
                "uv",
                split_axis=0,
                concat_axis=0,
                tiled=True,
            ),
            "channel",
            split_axis=1,
            concat_axis=1,
            tiled=True,
        ),
    )
    local_slot = got_slot.reshape(-1) - lax.axis_index("channel") * group_tiles
    row_index = (got_chan.reshape(-1)[:, None] + chan_offsets[None, :]) * group_tiles + local_slot[
        :, None
    ]
    cell_grid = accumulate(received, row_index, channels * group_tiles)
    gridded = cell_grid.reshape(2, channels, group_tiles * pixels)
    weighted = jnp.einsum(
        "ij,rjc->ric", inv_cov, gridded, preferred_element_type=jnp.float32
    ).astype(jnp.bfloat16)
    dft_table = delay_table(channels)
    projected = jnp.einsum("ij,rjc->ric", dft_table, weighted, preferred_element_type=jnp.float32)
    spec_real = projected[0, :channels] + projected[1, channels:]
    spec_imag = projected[1, :channels] - projected[0, channels:]
    spectra = jnp.stack([spec_real, spec_imag])[None]
    paired = lax.all_to_all(spectra, "parity", split_axis=3, concat_axis=0, tiled=True)
    even_half = paired[0]
    odd_half = paired[1]
    cross_power = (even_half[0] * odd_half[0] + even_half[1] * odd_half[1]) / channels
    differ = even_half - odd_half
    diff_power = (differ[0] * differ[0] + differ[1] * differ[1]) / channels
    return (cross_power, diff_power)


def solution(mesh):
    placed = (
        P("parity", "channel", "uv", None, None),
        P("parity", "channel", "uv", None, None),
        P("parity", "channel", "uv"),
        P("parity", "channel", "uv"),
        P(),
        P(),
    )
    return jax.shard_map(
        on_device,
        mesh=mesh,
        in_specs=placed,
        out_specs=(P(None, ("uv", "channel", "parity")), P(None, ("uv", "channel", "parity"))),
        check_vma=False,
    )
```

profile of v0, /device:TPU:0, one launch (start us, length us, event | category | flops | bytes accessed | tf_op | source)
XLA Modules:
  0.0 885.4 jit_solution(2845541411869033897)
XLA Ops:
  4.0 4.2 all-to-all-start.2
  10.3 1.8 all-to-all-done.2
  12.0 3.2 all-to-all-start
  15.9 3.2 all-to-all-done
  19.1 5.3 all-to-all-start.3
  24.4 2.1 fusion.38
  27.6 4.4 scatter_fusion
  31.9 3.5 all-to-all-start.4
  36.1 13.8 %all-to-all-done.4 = bf16[4,4,4,32,256]{4,3,2,1,0:T(8,128)(2,1)S(1)} async-done(((bf16[4,4,4,32,256]{4,3,2,1,0:T(8,128)(2,1)}), bf16[4,4,4,32,256]{4,3,2,1,0:T(8,128)(2,1)S(1)}, u32[]{:S(2)}, u32[]{:S(2)}) %all-to-all-start.4) | async-done | bytes 1048608 | tf_op jit(solution)/shard_map/all_to_all | solution.py:78
  49.9 5.1 all-to-all-start.1
  56.1 4.5 all-to-all-done.1
  60.6 3.5 all-to-all-start.5
  64.1 17.7 %sine_convert_fusion = (bf16[1024,1024]{1,0:T(8,128)(2,1)}, bf16[1024,1024]{1,0:T(8,128)(2,1)}) fusion(), kind=kLoop, calls=%fused_computation.41 | loop fusion | flops 16777216 | bytes 4194304 | tf_op jit(solution)/shard_map/convert.1
  82.0 6.4 all-to-all-done.5
  88.6 99.2 %while.11 = (s32[]{:T(128)}, bf16[32,2,512,256]{3,2,1,0:T(8,128)(2,1)}, s32[32]{0:T(128)S(1)}, bf16[2,1024,256]{2,1,0:T(8,128)(2,1)S(1)}, s32[64]{0:T(128)S(1)}, /*index=5*/s32[64]{0:T(128)S(1)}, s32[]{:T(128)}, s32[1]{0:T(128)}) while((s32[]{:T(128)}, bf16[32,2,512,256]{3,2,1,0:T(8,128)(2,1)}, s32[32]{0:T(128)S(1)}, ...), condition=%wide.region_8.9_spmd.clone, body=%wide.region_7.8_spmd.clone.sunk | while | flops 537661952 | bytes 1593981 | solution.py:29
  93.3 1.6 fusion.72
  96.4 1.6 fusion.72
  99.5 1.6 fusion.72
  105.6 1.6 fusion.72
  111.8 1.6 fusion.72
  118.0 1.6 fusion.72
  121.1 1.6 fusion.72
  124.2 1.6 fusion.72
  130.4 1.6 fusion.72
  136.6 1.6 fusion.72
  139.7 1.6 fusion.72
  142.8 1.6 fusion.72
  146.0 1.6 fusion.72
  152.2 1.6 fusion.72
  155.3 1.6 fusion.72
  161.5 1.6 fusion.72
  164.6 1.6 fusion.72
  167.7 1.6 fusion.72
  177.0 1.6 fusion.72
  180.1 1.6 fusion.72
  186.3 1.6 fusion.72
  187.9 13.7 %copy.43 = bf16[2,32,512,256]{3,2,1,0:T(8,128)(2,1)} copy(bf16[2,32,512,256]{3,2,0,1:T(8,128)(2,1)} %bitcast.113) | data formatting | bytes 33554432 | tf_op jit(solution)/shard_map/transpose | solution.py:30
  201.6 25.6 %reshape_reshape.3 = bf16[2,1024,4096]{2,1,0:T(8,128)(2,1)} reshape(bf16[2,32,512,256]{3,2,1,0:T(8,128)(2,1)} %copy.43) | data formatting | bytes 33554432 | tf_op jit(solution)/shard_map/reshape;reshape | solution.py:122
  227.2 27.0 %fusion.65 = bf16[2,1024,4096]{1,2,0:T(8,128)(2,1)} fusion(bf16[2,1024,4096]{2,1,0:T(8,128)(2,1)} %reshape_reshape.3, bf16[1024,1024]{1,0:T(8,128)(2,1)S(1)} %copy-done), kind=kOutput, calls=%fused_computation.19.clone.2 | convolution fusion | flops 17188257792 | bytes 35651584 | tf_op jit(solution)/shard_map/ij,rjc->ric/dot_general | solution.py:123
  254.3 43.4 %convolution_bitcast_fusion = f32[2,2048,4096]{1,2,0:T(8,128)} fusion(bf16[1024,1024]{1,0:T(8,128)(2,1)} %get-tuple-element.62, bf16[1024,1024]{1,0:T(8,128)(2,1)} %get-tuple-element.63, bf16[2,1024,4096]{1,2,0:T(8,128)(2,1)} %fusion.65), kind=kOutput, calls=%fused_computation.15 | convolution fusion | flops 34368126976 | bytes 88080384 | tf_op jit(solution)/shard_map/ij,rjc->ric/dot_general | solution.py:127
  297.7 34.1 %slice_add_fusion = (f32[1,1024,4096]{1,2,0:T(8,128)}, f32[1,1024,4096]{1,2,0:T(8,128)}) fusion(f32[2,2048,4096]{1,2,0:T(8,128)} %convolution_bitcast_fusion), kind=kLoop, calls=%fused_computation.18 | loop fusion | flops 8388608 | bytes 100663296 | tf_op jit(solution)/shard_map/add | solution.py:128
  331.7 23.5 %maximum_bitcast_fusion = f32[1,2,1024,4096]{2,3,1,0:T(8,128)} fusion(f32[1,1024,4096]{1,2,0:T(8,128)} %get-tuple-element.61, f32[1,1024,4096]{1,2,0:T(8,128)} %get-tuple-element.60), kind=kLoop, calls=%fused_computation.14 | loop fusion | flops 8388608 | bytes 67108864 | tf_op jit(solution)/shard_map/broadcast_in_dim | solution.py:130
  355.2 55.0 %copy.45 = f32[1,2,1024,4096]{2,1,0,3:T(2,128)} copy(f32[1,2,1024,4096]{2,3,1,0:T(8,128)} %maximum_bitcast_fusion) | data formatting | bytes 67108864 | tf_op jit(solution)/shard_map/broadcast_in_dim | solution.py:130
  410.2 393.8 %all_to_all.45 = f32[1,2,1024,4096]{2,1,0,3:T(2,128)} all-to-all(f32[1,2,1024,4096]{2,1,0,3:T(2,128)} %copy.45), channel_id=1, replica_groups=mesh['uv'=4,'channel'=4,'parity'=2] {'parity'}, dimensions={3} | all-to-all | bytes 67108864 | tf_op jit(solution)/shard_map/all_to_all | solution.py:131
  804.0 48.8 %copy.46 = f32[1,2,1024,2,2048]{4,2,1,0,3:T(8,128)} copy(f32[1,2,1024,2,2048]{2,1,4,3,0:T(2,128)} %bitcast.112) | data formatting | bytes 67108864 | tf_op jit(solution)/shard_map/all_to_all | solution.py:131
  852.8 16.5 %fusion.25 = f32[1024,2048]{1,0:T(8,128)} fusion(f32[2,1,2,1024,2048]{4,3,2,1,0:T(8,128)} %bitcast.110), kind=kLoop, calls=%fused_computation.30 | loop fusion | flops 8388608 | bytes 41943040 | tf_op jit(solution)/shard_map/div | solution.py:134
  869.3 11.8 %slice_subtract_fusion = f32[1,1,2,1024,2048]{4,3,2,1,0:T(8,128)S(1)} fusion(f32[2,1,2,1024,2048]{4,3,2,1,0:T(8,128)} %bitcast.111), kind=kLoop, calls=%fused_computation.16 | loop fusion | flops 4194304 | bytes 50331648 | tf_op jit(solution)/shard_map/sub | solution.py:135
  881.1 4.3 fusion.22
  (167 shorter events, 52.5 us)
Async XLA Ops:
  0.6 226.6 %copy-start = (bf16[1024,1024]{1,0:T(8,128)(2,1)S(1)}, bf16[1024,1024]{1,0:T(8,128)(2,1)}, u32[]{:S(2)}) copy-start(bf16[1024,1024]{1,0:T(8,128)(2,1)} %param.13) | copy-start | bytes 6291460
  4.0 8.1 all-to-all-start.2
  12.0 7.0 all-to-all-start
  19.1 12.9 %all-to-all-start.3 = ((s32[4,4,4]{2,0,1:T(4,128)}), s32[4,4,4]{2,0,1:T(4,128)S(1)}, u32[]{:S(2)}, u32[]{:S(2)}) async-start(s32[4,4,4]{2,0,1:T(4,128)} %copy.41), calls=%async_computation.3 | async-start | bytes 16384 | tf_op jit(solution)/shard_map/all_to_all | solution.py:90
  31.9 18.0 %all-to-all-start.4 = ((bf16[4,4,4,32,256]{4,3,2,1,0:T(8,128)(2,1)}), bf16[4,4,4,32,256]{4,3,2,1,0:T(8,128)(2,1)S(1)}, u32[]{:S(2)}, u32[]{:S(2)}) async-start(bf16[4,4,4,32,256]{4,3,2,1,0:T(8,128)(2,1)} %bitcast.7), calls=%async_computation.4 | async-start | bytes 2097152 | tf_op jit(solution)/shard_map/all_to_all | solution.py:78
  49.9 10.7 %all-to-all-start.1 = ((s32[4,4,4]{2,0,1:T(4,128)}), s32[4,4,4]{2,0,1:T(4,128)S(1)}, u32[]{:S(2)}, u32[]{:S(2)}) async-start(s32[4,4,4]{2,0,1:T(4,128)} %copy.39), calls=%async_computation.1 | async-start | bytes 16384 | tf_op jit(solution)/shard_map/all_to_all | solution.py:103
  60.6 27.9 %all-to-all-start.5 = ((bf16[4,4,4,32,256]{4,3,2,0,1:T(8,128)(2,1)}), bf16[4,4,4,32,256]{4,3,2,0,1:T(8,128)(2,1)S(1)}, u32[]{:S(2)}, u32[]{:S(2)}) async-start(bf16[4,4,4,32,256]{4,3,2,0,1:T(8,128)(2,1)} %copy.36), calls=%async_computation.5 | async-start | bytes 2097152 | tf_op jit(solution)/shard_map/all_to_all | solution.py:77
  869.3 16.1 %copy-start.1 = (bf16[1024,1024]{1,0:T(8,128)(2,1)S(1)}, bf16[1024,1024]{1,0:T(8,128)(2,1)}, u32[]{:S(2)}) copy-start(bf16[1024,1024]{1,0:T(8,128)(2,1)} %param.13) | copy-start | bytes 6291460
where the time goes:
time: 889 us; the launch traced here: 885 us
  blocking collectives  394 us (44%)
  local copies, waits for them, and re-layouts  178 us (20%)
  matrix products  123 us (14%)
  other arithmetic  113 us (13%)
  waiting for transfers between devices  29.7 us (3%)
  starting transfers between devices  24.9 us (3%)
  loops' own time  22.7 us (3%)
    all_to_all x1, blocking collectives, on_device(): lax.all_to_all(spectra, 'parity', split_axis=3, concat_axis=0, tiled=True)  394 us
    broadcast_in_dim x1, local copies, waits for them, and re-layouts, on_device(): spectra = jnp.stack([spec_real, spec_imag])[None]  55 us
    dot_general x32, matrix products, grid_block(): jnp.einsum('nm,rmp->rnp', onehot, values, preferred_element_type=jnp.floa...  50.2 us
    all_to_all x1, local copies, waits for them, and re-layouts, on_device(): lax.all_to_all(spectra, 'parity', split_axis=3, concat_axis=0, tiled=True)  48.8 us
    dot_general x1, matrix products, on_device(): jnp.einsum('ij,rjc->ric', dft_table, weighted, preferred_element_type=jnp...  43.4 us
    add x1, other arithmetic, on_device(): spec_real = projected[0, :channels] + projected[1, channels:]  34.1 us
    dot_general x1, matrix products, on_device(): jnp.einsum('ij,rjc->ric', inv_cov, gridded, preferred_element_type=jnp.fl...  27 us
    another operation x1, local copies, waits for them, and re-layouts, on_device(): gridded = cell_grid.reshape(2, channels, group_tiles * pixels)  25.6 us
  transfers between devices with their start and end apart: 6, of which 5 were waited for; matrix products, arithmetic and copies ran while one was open for 3% of the time, Pallas kernels for 0%

commit v1 on v0

v1 whole, which is shorter than its diff:
```python
import functools
import math

import jax
import jax.numpy as jnp
import ml_dtypes
import numpy as np
from jax import lax
from jax.experimental import pallas as pl
from jax.experimental.pallas import tpu as pltpu
from jax.sharding import PartitionSpec as P

MESH = pl.DeviceIdType.MESH


def half_table(count):
    half = count // 2
    phase = np.arange(half + 1)[:, None] * np.arange(count)[None, :] % count
    angles = phase.astype(np.float64) * (2.0 * math.pi / count)
    rows = np.concatenate([np.cos(angles[:half]), np.cos(angles[half:]), np.sin(angles[1:half])])
    return (rows.astype(np.float32).astype(ml_dtypes.bfloat16).astype(np.float32) / count).astype(
        ml_dtypes.bfloat16
    )


def pack_kernel(n_ch, slots, group_tiles, channels, tile, chan, owner, vis, ker, out, meta, slot_of, own_count, dest_count):
    blocks = vis.shape[0]
    dests = meta.shape[0]
    chan_base = lax.axis_index("channel") * (channels // n_ch)
    for index in range(own_count.shape[0]):
        own_count[index] = 0

    def clear(dest, _):
        dest_count[dest] = 0
        for rank in range(slots):
            meta[dest, 0, rank] = -1
        return 0

    lax.fori_loop(0, dests, clear, 0)

    def number(index, _):
        holder = owner[index]
        place = own_count[holder]
        slot_of[index] = place
        own_count[holder] = place + 1
        return 0

    lax.fori_loop(0, owner.shape[0], number, 0, unroll=8)
    for block in range(blocks):
        where = tile[block]
        place = slot_of[where]
        dest = owner[where] * n_ch + place // group_tiles
        rank = dest_count[dest]
        dest_count[dest] = rank + 1
        meta[dest, 0, rank] = place * channels + chan_base + chan[block]
        out[dest, rank] = jnp.dot(vis[block], ker[block], preferred_element_type=jnp.float32).astype(out.dtype)


def exchange_kernel(n_uv, n_ch, data, meta, got, got_meta, keep_sem, send_sem, recv_sem, fsend_sem, frecv_sem):
    dests = n_uv * n_ch
    u, c, p = lax.axis_index("uv"), lax.axis_index("channel"), lax.axis_index("parity")
    me = u * n_ch + c
    partner = (u, c, 1 - p)

    def peer(step):
        dest = lax.rem(me + step, dests)
        return dest, (lax.div(dest, n_ch), lax.rem(dest, n_ch), p)

    barrier = pltpu.get_barrier_semaphore()
    pl.semaphore_signal(barrier, inc=1, device_id=partner, device_id_type=MESH)

    def greet(step, _):
        pl.semaphore_signal(barrier, inc=1, device_id=peer(step)[1], device_id_type=MESH)
        return 0

    lax.fori_loop(1, dests, greet, 0)
    pl.semaphore_wait(barrier, dests)

    def copies(step, source, landing, sends, recvs, device):
        return [
            pltpu.make_async_remote_copy(
                src_ref=values,
                dst_ref=target,
                send_sem=sends.at[kind, step],
                recv_sem=recvs.at[kind, step],
                device_id=device,
                device_id_type=MESH,
            )
            for kind, (values, target) in enumerate(zip(source, landing))
        ]

    def outward(step):
        dest, device = peer(step)
        return copies(
            step, (data.at[dest], meta.at[dest]), (got.at[p, me], got_meta.at[p, me]), send_sem, recv_sem, device
        )

    def onward(step):
        origin = lax.rem(me + dests - step, dests)
        held = (got.at[p, origin], got_meta.at[p, origin])
        return copies(step, held, held, fsend_sem, frecv_sem, partner)

    def first_send(step, _):
        for copy in outward(step):
            copy.start()
        return 0

    lax.fori_loop(1, dests, first_send, 0)
    kept = [
        pltpu.make_async_copy(data.at[me], got.at[p, me], keep_sem.at[0]),
        pltpu.make_async_copy(meta.at[me], got_meta.at[p, me], keep_sem.at[1]),
    ]
    for copy in kept:
        copy.start()
    for copy in kept:
        copy.wait()
    for copy in onward(0):
        copy.start()

    def forward(step, _):
        for copy in outward(step):
            copy.wait_recv()
        for copy in onward(step):
            copy.start()
        return 0

    lax.fori_loop(1, dests, forward, 0)

    def finish(step, _):
        for copy in outward(step):
            copy.wait_send()
        return 0

    lax.fori_loop(1, dests, finish, 0)

    def close(step, _):
        for copy in onward(step):
            copy.wait()
        return 0

    lax.fori_loop(0, dests, close, 0)


def power_kernel(n_ch, slots, dests, tiles, scale, meta, got, mix, cross, diff, acc, grid, high, count, listing):
    step = pl.program_id(0)
    channels = mix.shape[0]
    half = channels // 2
    pixels = cross.shape[1]
    width = got.shape[1] // 2
    capacity = dests * slots
    window = 2 * width

    @pl.when(step == 0)
    def _():
        acc[...] = jnp.zeros_like(acc)
        grid[...] = jnp.zeros_like(grid)
        base = (lax.axis_index("channel") * 2 + lax.axis_index("parity")) * tiles
        for index in range(2 * tiles):
            count[index] = 0
        for parity in range(2):

            def scan(origin, _):
                for rank in range(slots):
                    entry = meta[parity, origin, 0, rank]
                    local = lax.div(entry, channels) - base

                    @pl.when((entry >= 0) & (local >= 0) & (local < tiles))
                    def _():
                        row = local * 2 + parity
                        at = count[row]
                        count[row] = at + 1
                        place = (parity * dests + origin) * slots + rank
                        listing[row * capacity + at] = place * channels + lax.rem(entry, channels)

                return 0

            lax.fori_loop(0, dests, scan, 0)

    def where(parity, index):
        entry = listing[(step * 2 + parity) * capacity + index]
        first = lax.rem(entry, channels)
        aligned = jnp.minimum(lax.div(first, width) * width, channels - window)
        aligned = pl.multiple_of(aligned, width)
        return lax.div(entry, channels), first - aligned, aligned

    for parity in range(2):
        total = count[step * 2 + parity]

        def add(index, _):
            place, shift, aligned = where(parity, index)
            block = got[place].astype(jnp.float32) * scale
            filler = jnp.zeros((window - width, pixels), jnp.float32)
            for part in range(2):
                moved = pltpu.roll(
                    jnp.concatenate([block[part * width : (part + 1) * width], filler], axis=0), shift, 0
                )
                columns = slice(part * pixels, (part + 1) * pixels)
                acc[pl.ds(aligned, window), columns] += moved
            return 0

        lax.fori_loop(0, total, add, 0)

        def keep(index, _):
            _, _, aligned = where(parity, index)
            columns = slice(2 * parity * pixels, 2 * (parity + 1) * pixels)
            grid[pl.ds(aligned, window), columns] = acc[pl.ds(aligned, window), :].astype(grid.dtype)
            return 0

        lax.fori_loop(0, total, keep, 0)

        def wipe(index, _):
            _, _, aligned = where(parity, index)
            acc[pl.ds(aligned, window), :] = jnp.zeros((window, 2 * pixels), jnp.float32)
            return 0

        lax.fori_loop(0, total, wipe, 0)

    rows = math.gcd(half, 128)

    def powers(spec):
        even_real, even_imag, odd_real, odd_imag = spec
        real_gap, imag_gap = even_real - odd_real, even_imag - odd_imag
        return even_real * odd_real + even_imag * odd_imag, real_gap * real_gap + imag_gap * imag_gap

    for start in range(0, half, rows):
        cosine = jnp.dot(mix[start : start + rows, :], grid[...], preferred_element_type=jnp.float32)
        sine = jnp.dot(mix[half + start : half + start + rows, :], grid[...], preferred_element_type=jnp.float32)
        cos_parts = [cosine[:, k * pixels : (k + 1) * pixels] for k in range(4)]
        sin_parts = [sine[:, k * pixels : (k + 1) * pixels] for k in range(4)]
        if start == 0:
            ends = powers([part[:8] for part in sin_parts])
            high[0, half : half + 8, :] = ends[0]
            high[1, half : half + 8, :] = ends[1]
            first = lax.broadcasted_iota(jnp.int32, (rows, pixels), 0) == 0
            sin_parts = [jnp.where(first, 0.0, part) for part in sin_parts]
        low, top = [], []
        for parity in range(2):
            cr, ci = cos_parts[2 * parity : 2 * parity + 2]
            sr, si = sin_parts[2 * parity : 2 * parity + 2]
            low += [cr + si, ci - sr]
            top += [cr - si, ci + sr]
        low_powers = powers(low)
        cross[start : start + rows, :] = low_powers[0]
        diff[start : start + rows, :] = low_powers[1]
        top_powers = powers(top)
        high[0, start : start + rows, :] = top_powers[0]
        high[1, start : start + rows, :] = top_powers[1]

    backwards = 7 - lax.broadcasted_iota(jnp.int32, (8, pixels), 0)
    for row in range(0, half, 8):
        for which, target in enumerate((cross, diff)):
            piece = high[which, half - row - 7 : half - row + 1, :]
            target[half + row : half + row + 8, :] = jnp.take_along_axis(piece, backwards, axis=0)

    for parity in range(2):

        def clean(index, _):
            _, _, aligned = where(parity, index)
            columns = slice(2 * parity * pixels, 2 * (parity + 1) * pixels)
            grid[pl.ds(aligned, window), columns] = jnp.zeros((window, 2 * pixels), grid.dtype)
            return 0

        lax.fori_loop(0, count[step * 2 + parity], clean, 0)


def on_device(visibility, kernel, block_tile, block_chan, tile_owner, inv_cov):
    n_uv = lax.axis_size("uv")
    n_ch = lax.axis_size("channel")
    n_par = lax.axis_size("parity")
    samples = visibility[0, 0]
    weights = kernel[0, 0]
    blocks, doubled, _ = samples.shape
    pixels = weights.shape[2]
    channels = inv_cov.shape[0]
    tile_total = tile_owner.shape[0]
    group_tiles = tile_total // n_uv // n_ch
    out_tiles = group_tiles // n_par
    dests = n_uv * n_ch
    slots = max(1, 2 * blocks // dests)
    smem = pl.BlockSpec(memory_space=pltpu.SMEM)
    vmem = pl.BlockSpec(memory_space=pltpu.VMEM)
    anywhere = pl.BlockSpec(memory_space=pl.ANY)

    mix = jnp.dot(half_table(channels), inv_cov, preferred_element_type=jnp.float32).astype(jnp.bfloat16)

    outgoing, meta = pl.pallas_call(
        functools.partial(pack_kernel, n_ch, slots, group_tiles, channels),
        out_shape=(
            jax.ShapeDtypeStruct((dests, slots, doubled, pixels), jnp.bfloat16),
            jax.ShapeDtypeStruct((dests, 1, 128), jnp.int32),
        ),
        in_specs=[smem, smem, smem, vmem, vmem],
        out_specs=(vmem, smem),
        scratch_shapes=[
            pltpu.SMEM((tile_total,), jnp.int32),
            pltpu.SMEM((n_uv,), jnp.int32),
            pltpu.SMEM((dests,), jnp.int32),
        ],
        compiler_params=pltpu.CompilerParams(vmem_limit_bytes=32 << 20),
        name="pack_terms",
    )(block_tile[0, 0], block_chan[0, 0], tile_owner, samples, weights)

    got, got_meta = pl.pallas_call(
        functools.partial(exchange_kernel, n_uv, n_ch),
        out_shape=(
            jax.ShapeDtypeStruct((2, dests, slots, doubled, pixels), jnp.bfloat16),
            jax.ShapeDtypeStruct((2, dests, 1, 128), jnp.int32),
        ),
        in_specs=[vmem, vmem],
        out_specs=(vmem, vmem),
        scratch_shapes=[
            pltpu.SemaphoreType.DMA((2,)),
            pltpu.SemaphoreType.DMA((2, dests)),
            pltpu.SemaphoreType.DMA((2, dests)),
            pltpu.SemaphoreType.DMA((2, dests)),
            pltpu.SemaphoreType.DMA((2, dests)),
        ],
        compiler_params=pltpu.CompilerParams(
            collective_id=0, has_side_effects=True, vmem_limit_bytes=32 << 20
        ),
        name="exchange_terms",
    )(outgoing, meta)

    area = pl.BlockSpec((channels, pixels), lambda t: (0, t))
    return pl.pallas_call(
        functools.partial(power_kernel, n_ch, slots, dests, out_tiles, math.sqrt(channels)),
        grid=(out_tiles,),
        out_shape=(jax.ShapeDtypeStruct((channels, out_tiles * pixels), jnp.float32),) * 2,
        in_specs=[smem, vmem, vmem],
        out_specs=(area, area),
        scratch_shapes=[
            pltpu.VMEM((channels, 2 * pixels), jnp.float32),
            pltpu.VMEM((channels, 4 * pixels), jnp.bfloat16),
            pltpu.VMEM((2, channels // 2 + 8, pixels), jnp.float32),
            pltpu.SMEM((2 * out_tiles,), jnp.int32),
            pltpu.SMEM((2 * out_tiles * dests * slots,), jnp.int32),
        ],
        compiler_params=pltpu.CompilerParams(vmem_limit_bytes=48 << 20),
        name="power_spectra",
    )(got_meta, got.reshape(2 * dests * slots, doubled, pixels), mix)


def solution(mesh):
    placed = (
        P("parity", "channel", "uv", None, None),
        P("parity", "channel", "uv", None, None),
        P("parity", "channel", "uv"),
        P("parity", "channel", "uv"),
        P(),
        P(),
    )
    return jax.shard_map(
        on_device,
        mesh=mesh,
        in_specs=placed,
        out_specs=(P(None, ("uv", "channel", "parity")), P(None, ("uv", "channel", "parity"))),
        check_vma=False,
    )
```

time: 889 us -> 81.1 us (0.09)
  blocking collectives: 394 us -> 0 us
  local copies, waits for them, and re-layouts: 178 us -> 4.68 us
  matrix products: 123 us -> 2.33 us
  other arithmetic: 113 us -> 0 us
  Pallas kernels: 0 us -> 72.7 us
  waiting for transfers between devices: 29.7 us -> 0 us
  starting transfers between devices: 24.9 us -> 0 us
  loops' own time: 22.7 us -> 0 us
    all_to_all x1 -> x0, blocking collectives: 394 us -> none  [on_device(): lax.all_to_all(spectra, 'parity', split_axis=3, concat_axis=0, tiled=True)]
    dot_general x35 -> x1, matrix products: 123 us -> 2.33 us  [on_device(): jnp.dot(half_table(channels), inv_cov, preferred_element_type=jnp.float32)]
    pallas_call x0 -> x3, Pallas kernels: none -> 72.7 us  [the longest x1 38.5 us: on_device(): pl.pallas_call(functools.partial(exchange_kernel, n_uv, n_ch), out_shape=...]
    broadcast_in_dim x2 -> x0, local copies, waits for them, and re-layouts: 56.1 us -> none  [the longest x1 55 us: on_device(): spectra = jnp.stack([spec_real, spec_imag])[None]]
    all_to_all x6 -> x0, local copies, waits for them, and re-layouts: 51.1 us -> none  [the longest x1 48.8 us: on_device(): lax.all_to_all(spectra, 'parity', split_axis=3, concat_axis=0, tiled=True)]
    add x35 -> x0, other arithmetic: 34.9 us -> none  [the longest x1 34.1 us: on_device(): spec_real = projected[0, :channels] + projected[1, channels:]]
    all_to_all x6 -> x0, waiting for transfers between devices: 29.7 us -> none  [the longest x1 13.8 us: on_device(): lax.all_to_all(outgoing.reshape(uv_count, chan_count, slot_count, doubled...]
    another operation x1 -> x0, local copies, waits for them, and re-layouts: 25.6 us -> none  [on_device(): gridded = cell_grid.reshape(2, channels, group_tiles * pixels)]
  transfers between devices with their start and end apart: 6 -> 0, of which waited for: 5 -> 0; matrix products, arithmetic and copies ran while one was open for 3% -> 0% of each run, Pallas kernels for 0% -> 0%
where the time goes in v1:
time: 81.1 us; the launch traced here: 80.4 us
  Pallas kernels  72.7 us (90%)
  local copies, waits for them, and re-layouts  4.68 us (6%)
  matrix products  2.33 us (3%)
    pallas_call x1, Pallas kernels, on_device(): pl.pallas_call(functools.partial(exchange_kernel, n_uv, n_ch), out_shape=...  38.5 us
    pallas_call x1, Pallas kernels, on_device(): pl.pallas_call(functools.partial(power_kernel, n_ch, slots, dests, out_ti...  31.1 us
    unnamed x14, local copies, waits for them, and re-layouts  4.68 us
    pallas_call x1, Pallas kernels, on_device(): pl.pallas_call(functools.partial(pack_kernel, n_ch, slots, group_tiles, c...  3.1 us
    dot_general x1, matrix products, on_device(): jnp.dot(half_table(channels), inv_cov, preferred_element_type=jnp.float32)  2.33 us

profile of v1, /device:TPU:0, one launch (start us, length us, event | category | flops | bytes accessed | tf_op | source)
XLA Modules:
  0.0 80.4 jit_solution(9444601952249375052)
XLA Ops:
  0.6 0.0 copy-start
  0.6 0.0 copy-start.1
  0.7 1.7 %copy-done.1 = bf16[1,1,32,128,256]{4,3,2,1,0:T(8,128)(2,1)S(1)} copy-done((bf16[1,1,32,128,256]{4,3,2,1,0:T(8,128)(2,1)S(1)}, bf16[1,1,32,128,256]{4,3,2,1,0:T(8,128)(2,1)}, u32[]{:S(2)}) %copy-start.1) | copy-done | bytes 2097176
  2.4 0.0 copy-start.2
  2.4 0.9 %copy-done.2 = bf16[1,1,32,32,128]{4,3,2,1,0:T(8,128)(2,1)S(1)} copy-done((bf16[1,1,32,32,128]{4,3,2,1,0:T(8,128)(2,1)S(1)}, bf16[1,1,32,32,128]{4,3,2,1,0:T(8,128)(2,1)}, u32[]{:S(2)}) %copy-start.2) | copy-done | bytes 262168
  3.3 0.0 copy-start.3
  3.3 0.7 copy-done.3
  4.0 0.0 copy-start.4
  4.0 0.7 copy-done.4
  4.7 0.0 copy-start.5
  4.7 0.7 copy-done.5
  5.3 0.0 copy-start.6
  5.3 3.1 %pack_terms.1 = (bf16[16,4,32,256]{3,2,1,0:T(8,128)(2,1)S(1)}, s32[16,1,128]{2,1,0:T(1,128)S(1)}) custom-call(s32[32]{0:T(128)S(1)} %bitcast.10, s32[32]{0:T(128)S(1)} %bitcast.11, s32[256]{0:T(256)S(1)} %copy-done.3, bf16[32,32,128]{2,1,0:T(8,128)(2,1)S(1)} %bitcast.9, bf16[32,128,256]{2,1,0:T(8,128)(2,1)S(1)} %bitcast.7), custom_call_target="tpu_custom_call" | custom-call | tf_op jit(solution)/shard_map/pack_terms/pallas_call | solution.py:286
  8.4 38.5 %exchange_terms.1 = (bf16[2,16,4,32,256]{4,3,2,1,0:T(8,128)(2,1)S(1)}, s32[2,16,1,128]{3,2,1,0:T(1,128)S(1)}) custom-call(bf16[16,4,32,256]{3,2,1,0:T(8,128)(2,1)S(1)} %get-tuple-element.6.data, s32[16,1,128]{2,1,0:T(1,128)S(1)} %get-tuple-element.7.meta), custom_call_target="tpu_custom_call" | custom-call | tf_op jit(solution)/shard_map/exchange_terms/pallas_call | solution.py:303
  46.9 0.0 copy-done
  46.9 0.0 copy-done.6
  46.9 2.3 %convolution_convert_fusion.mix = bf16[1024,1024]{1,0:T(8,128)(2,1)S(1)} fusion(bf16[1024,1024]{1,0:T(8,128)(2,1)S(1)} %copy-done.6, bf16[1024,1024]{1,0:T(8,128)(2,1)S(1)} %copy-done), kind=kOutput, calls=%fused_computation | convolution fusion | flops 2148532224 | bytes 6291456 | tf_op jit(solution)/shard_map/dot_general | solution.py:284
  49.3 31.1 %power_spectra.1 = (f32[1024,2048]{1,0:T(8,128)}, f32[1024,2048]{1,0:T(8,128)}) custom-call(s32[2,16,1,128]{3,2,1,0:T(1,128)S(1)} %get-tuple-element.8.meta, bf16[128,32,256]{2,1,0:T(8,128)(2,1)S(1)} %bitcast.8, bf16[1024,1024]{1,0:T(8,128)(2,1)S(1)} %convolution_convert_fusion.mix), custom_call_target="tpu_custom_call" | custom-call | tf_op jit(solution)/shard_map/power_spectra/pallas_call | solution.py:325
Async XLA Ops:
  0.6 46.3 %copy-start = (bf16[1024,1024]{1,0:T(8,128)(2,1)S(1)}, bf16[1024,1024]{1,0:T(8,128)(2,1)}, u32[]{:S(2)}) copy-start(bf16[1024,1024]{1,0:T(8,128)(2,1)} %param.12) | copy-start | bytes 6291460
  0.6 1.7 %copy-start.1 = (bf16[1,1,32,128,256]{4,3,2,1,0:T(8,128)(2,1)S(1)}, bf16[1,1,32,128,256]{4,3,2,1,0:T(8,128)(2,1)}, u32[]{:S(2)}) copy-start(bf16[1,1,32,128,256]{4,3,2,1,0:T(8,128)(2,1)} %param.8) | copy-start | bytes 6291460
  2.4 0.9 %copy-start.2 = (bf16[1,1,32,32,128]{4,3,2,1,0:T(8,128)(2,1)S(1)}, bf16[1,1,32,32,128]{4,3,2,1,0:T(8,128)(2,1)}, u32[]{:S(2)}) copy-start(bf16[1,1,32,32,128]{4,3,2,1,0:T(8,128)(2,1)} %param.7) | copy-start | bytes 786436
  3.3 0.7 copy-start.3
  4.0 0.7 copy-start.4
  4.7 0.7 copy-start.5
  5.3 41.6 %copy-start.6 = (bf16[1024,1024]{1,0:T(8,128)(2,1)S(1)}, bf16[1024,1024]{1,0:T(8,128)(2,1)}, u32[]{:S(2)}) copy-start(bf16[1024,1024]{1,0:T(8,128)(2,1)} %constant.2.clone) | copy-start | bytes 6291460
